TPU v7x, 512 devices: a whole 4x8x8 slice. The times are simulated.
512 devices in a mesh: row: 16 (over y, core), col: 32 (over z, x).
Axes of the slice: x: 4, y: 8, z: 8, core: 2. Of those that a mesh axis runs over, the one named last changes fastest.
Arguments:
- matrix: bfloat16 [8192, 57344], P('row', 'col'), may hold values from -6 to 6
- lower_inv: float32 [2, 256, 256], replicated, may hold values from -1 to 1, as said below
- upper_inv: float32 [2, 256, 256], replicated, may hold values from -0.12 to 0.12, as said below
Outputs:
- factored: bfloat16 [8192, 57344], P('row', 'col')
Inputs may be any that keep to these rules, and one draw needn't show every extreme that they name: `lower_inv`: ones on the diagonal and zeros above it. `upper_inv`: zeros below the diagonal; the diagonal is positive.
All inputs are finite; a program needn't handle non-finite values.
Results may differ from a plain program's by a relative error of at most 0.0069.
Values may be sent and summed in bfloat16 or wider, within the bound.
A program may use at most 64 MiB of HBM per device.

v0:
```python
import jax
import jax.numpy as jnp
from jax import lax
from jax.sharding import PartitionSpec as P


def spread(block, axis, source):
    block = jnp.where(lax.axis_index(axis) == source, block, jnp.zeros_like(block))
    return lax.psum(block, axis)


def factor_panel(column, top_rows, section, row_block, col_block, lower_inv, upper_inv):

    def solve_left():
        return jnp.dot(
            column,
            upper_inv[section],
            precision=lax.Precision.HIGHEST,
            preferred_element_type=jnp.float32,
        )

    def empty_left():
        return jnp.zeros(column.shape, jnp.float32)

    lower_part = lax.cond(lax.axis_index("col") == section, solve_left, empty_left)
    lower_part = jnp.where((row_block > section)[:, None], lower_part, 0.0).astype(jnp.bfloat16)
    lower_part = spread(lower_part, "col", section)

    def solve_top():
        return jnp.dot(
            lower_inv[section],
            top_rows,
            precision=lax.Precision.HIGHEST,
            preferred_element_type=jnp.float32,
        )

    def empty_top():
        return jnp.zeros(top_rows.shape, jnp.float32)

    upper_part = lax.cond(lax.axis_index("row") == section, solve_top, empty_top)
    upper_part = jnp.where((col_block > section)[None, :], upper_part, 0.0).astype(jnp.bfloat16)
    upper_part = spread(upper_part, "row", section)
    return (lower_part, upper_part)


def body(matrix, lower_inv, upper_inv):
    width = upper_inv.shape[1]
    row_count, col_count = matrix.shape
    row_block = jnp.arange(row_count, dtype=jnp.int32) // width * lax.axis_size(
        "row"
    ) + lax.axis_index("row")
    col_block = jnp.arange(col_count, dtype=jnp.int32) // width * lax.axis_size(
        "col"
    ) + lax.axis_index("col")
    current = matrix.astype(jnp.float32)
    factors = []
    for section in range(2):
        lower_part, upper_part = factor_panel(
            current[:, :width],
            current[:width, :],
            section,
            row_block,
            col_block,
            lower_inv,
            upper_inv,
        )
        current = current - jnp.dot(lower_part, upper_part, preferred_element_type=jnp.float32)
        factors.append((lower_part, upper_part))
    for section in range(2):
        lower_part, upper_part = factors[section]
        left_cols = jnp.where(
            (lax.axis_index("col") == section) & (row_block > section)[:, None],
            lower_part.astype(jnp.float32),
            current[:, :width],
        )
        current = current.at[:, :width].set(left_cols)
        top_cols = jnp.where(
            (lax.axis_index("row") == section) & (col_block > section)[None, :],
            upper_part.astype(jnp.float32),
            current[:width, :],
        )
        current = current.at[:width, :].set(top_cols)
    return current.astype(jnp.bfloat16)


def solution(mesh):
    in_specs = (P("row", "col"), P(), P())
    out_specs = P("row", "col")
    return jax.shard_map(body, mesh=mesh, in_specs=in_specs, out_specs=out_specs, check_vma=False)
```

profile of v0, /device:TPU:1, one launch (start us, length us, event | category | flops | bytes accessed | tf_op | source)
XLA Modules:
  0.0 578.9 jit_solution(1544542693724781113)
XLA Ops:
  6.5 3.6 convert_element_type.42
  10.2 1.7 conditional.4
  10.2 1.7 fusion
  11.9 0.9 fusion.22
  12.8 0.1 conditional.5
  12.9 0.1 broadcast.345
  12.9 1.1 fusion.18
  14.1 0.0 all-reduce.9.cloned.1.call-start
  14.2 153.6 %all-reduce.5.cloned.1.call-done = bf16[512,256]{1,0:T(8,128)(2,1)} async-done(((bf16[512,256]{1,0:T(8,128)(2,1)}), bf16[512,256]{1,0:T(8,128)(2,1)}) %all-reduce.5.cloned.1.call-update) | async-done | bytes 262160 | tf_op jit(solution)/shard_map/psum | solution.py:9
  167.8 119.6 %all-reduce.7.cloned.1.call-done = bf16[256,1792]{1,0:T(8,128)(2,1)} async-done(((bf16[256,1792]{1,0:T(8,128)(2,1)}), bf16[256,1792]{1,0:T(8,128)(2,1)}) %all-reduce.7.cloned.1.call-update) | async-done | bytes 917520 | tf_op jit(solution)/shard_map/psum | solution.py:9
  287.4 3.7 convolution_subtract_fusion.1
  291.1 0.9 fusion.23
  292.1 3.2 conditional.7
  292.1 3.2 fusion.12
  295.3 1.1 fusion.19
  296.4 0.7 compare_reduce_fusion
  297.2 146.9 %all-reduce.9.cloned.1.call-done = bf16[512,256]{1,0:T(8,128)(2,1)} async-done(((bf16[512,256]{1,0:T(8,128)(2,1)}), bf16[512,256]{1,0:T(8,128)(2,1)}) %all-reduce.9.cloned.1.call-update) | async-done | bytes 262160 | tf_op jit(solution)/shard_map/psum | solution.py:9
  444.1 119.5 %all-reduce.11.cloned.1.call-done = bf16[256,1792]{1,0:T(8,128)(2,1)} async-done(((bf16[256,1792]{1,0:T(8,128)(2,1)}), bf16[256,1792]{1,0:T(8,128)(2,1)}) %all-reduce.11.cloned.1.call-update) | async-done | bytes 917520 | tf_op jit(solution)/shard_map/psum | solution.py:9
  563.6 3.0 convolution_subtract_fusion
  566.7 0.9 fusion.20
  567.6 0.3 fusion.17
  567.9 0.9 fusion.21
  568.8 1.2 copy-done
  570.0 2.3 fusion.16
  (32 shorter events, 0.3 us)
Async XLA Ops:
  6.5 161.3 %all-reduce.5.cloned.1.call-start = ((), (), s32[]{:S(2)}) async-start(), calls=%async_computation | async-start | bytes 524288 | tf_op jit(solution)/shard_map/psum | solution.py:9
  6.5 3.6 copy-start.7
  10.2 2.7 copy-start.6
  12.8 274.6 %all-reduce.7.cloned.1.call-start = ((), (), s32[]{:S(2)}) async-start(), calls=%async_computation.1 | async-start | bytes 1835008 | tf_op jit(solution)/shard_map/psum | solution.py:9
  12.9 274.5 %copy-start.1 = (bf16[512,1792]{1,0:T(8,128)(2,1)S(1)}, bf16[512,1792]{1,0:T(8,128)(2,1)}, u32[]{:S(2)}) copy-start(bf16[512,1792]{1,0:T(8,128)(2,1)} %param.19) | copy-start | bytes 5505028
  14.1 430.0 %all-reduce.9.cloned.1.call-start = ((), (), s32[]{:S(2)}) async-start(), calls=%async_computation.2 | async-start | bytes 524288 | tf_op jit(solution)/shard_map/psum | solution.py:9
  14.2 276.9 %copy-start.8 = (f32[2,256,256]{2,1,0:T(8,128)S(1)}, f32[2,256,256]{2,1,0:T(8,128)}, u32[]{:S(2)}) copy-start(f32[2,256,256]{2,1,0:T(8,128)} %param.21) | copy-start | bytes 1572868
  292.0 271.6 %all-reduce.11.cloned.1.call-start = ((), (), s32[]{:S(2)}) async-start(), calls=%async_computation.3 | async-start | bytes 1835008 | tf_op jit(solution)/shard_map/psum | solution.py:9
  297.1 269.5 %copy-start.4 = (bf16[512,256]{1,0:T(8,128)(2,1)S(1)}, bf16[512,256]{1,0:T(8,128)(2,1)}, u32[]{:S(2)}) copy-start(bf16[512,256]{1,0:T(8,128)(2,1)} %all-reduce.5.cloned.1.call-done) | copy-start | bytes 786436
  297.1 270.4 %copy-start.2 = (bf16[256,1792]{1,0:T(8,128)(2,1)S(1)}, bf16[256,1792]{1,0:T(8,128)(2,1)}, u32[]{:S(2)}) copy-start(bf16[256,1792]{1,0:T(8,128)(2,1)} %all-reduce.7.cloned.1.call-done) | copy-start | bytes 2752516
  566.6 1.3 copy-start.5
  567.6 2.4 copy-start.3
  568.8 1.2 copy-start
Sparse Core Ops, SparseCore 0:
  12.9 154.8 all-reduce.4
  170.1 117.1 all-reduce.6
  292.1 151.8 all-reduce.8
  446.4 117.1 all-reduce.10
where the time goes:
time: 579 us
  waiting for transfers between devices  540 us (93%)
  between operations  13.3 us (2%)
  other arithmetic  12.8 us (2%)
  matrix products  11.6 us (2%)
    psum x4, waiting for transfers between devices, spread(): return lax.psum(block, axis)  540 us
  transfers between devices with their start and end apart: 4, of which 4 were waited for; matrix products, arithmetic and copies ran while one was open for 1% of the time, Pallas kernels for 0%

commit v1 on v0

v1 whole, which is shorter than its diff:
```python
import functools

import jax
import jax.numpy as jnp
from jax import lax
from jax.experimental import pallas as pl
from jax.experimental.pallas import tpu as pltpu
from jax.sharding import PartitionSpec as P

MESH = pl.DeviceIdType.MESH
F32 = jnp.float32
BF16 = jnp.bfloat16
NB = 256
NY, NZ, NX = 8, 8, 4
HOP = 8

BOTH = {0: (2, 6), 2: (1, 3), 3: (4,), 6: (7, 5)}
CHAIN = {k: (k + 1,) for k in range(7)}
SKIP = {0: (2,), 2: (4, 1), 4: (6, 3), 6: (7, 5)}


def depths(tree):
    depth = {0: 0}
    todo = [0]
    while todo:
        k = todo.pop()
        for child in tree.get(k, ()):
            far = min((child - k) % 8, (k - child) % 8)
            depth[child] = depth[k] + HOP + (far - 1)
            todo.append(child)
    return [depth[k] for k in range(8)]


def offsets(tree, slot):
    out = []
    for k in range(8):
        children = tree.get(k, ())
        out.append((children[slot] - k + 4) % 8 - 4 if slot < len(children) else 0)
    return out


def lut(index, values):
    result = jnp.int32(values[0])
    for k in range(1, len(values)):
        if values[k] != values[0]:
            result = jnp.where(index == k, jnp.int32(values[k]), result)
    return result


GROUPS = ((BOTH, 4, 2), (CHAIN, 24, 1))
UCH = 28
LROWS = 64
LCH = 512 // LROWS
XCH = NB // LROWS


def split(value):
    high = value.astype(BF16)
    return high, (value - high.astype(F32)).astype(BF16)


def dot(a, b):
    return jnp.dot(a, b, preferred_element_type=F32)


def kernel(mat, linv, uinv, out, U, X, L, M, inv, LF, UF, work, l10, u01, us, ur, ps, pr, ls, lr, xs, xr, xp, xq, loc):
    r = lax.axis_index("row")
    c = lax.axis_index("col")
    y, core = r // 2, lax.rem(r, 2)
    z, x = c // NX, lax.rem(c, NX)
    sign = 1 - 2 * core
    p = lax.rem(NY + sign * y, NY)
    partner = (y * 2 + 1 - core, c)

    def at_y(off):
        return (lax.rem(y + off + NY, NY) * 2 + core, c)

    def at_z(off):
        return (r, lax.rem(z + off + NZ, NZ) * NX + x)

    def at_x(off):
        return (r, z * NX + lax.rem(x + off + NX, NX))

    barrier = pltpu.get_barrier_semaphore()
    near = [at_y(1), at_y(-1), at_y(2), at_y(-2), at_z(1), at_z(-1), at_z(2), at_z(-2), at_x(1), at_x(-1), partner]
    for device in near:
        pl.semaphore_signal(barrier, inc=1, device_id=device, device_id_type=MESH)

    local = [
        pltpu.make_async_copy(mat, M, loc.at[0]),
        pltpu.make_async_copy(linv, inv.at[0], loc.at[1]),
        pltpu.make_async_copy(uinv, inv.at[1], loc.at[2]),
    ]
    for copy in local:
        copy.start()
    own_rows = pltpu.make_async_copy(mat.at[pl.ds(0, NB)], U.at[core], loc.at[3])
    own_cols = pltpu.make_async_copy(mat.at[:, pl.ds(0, NB)], L.at[lax.rem(x, 2)], loc.at[4])
    src_u = p == 0
    src_l = c < 2

    @pl.when(src_u)
    def _():
        own_rows.start()

    @pl.when(src_l)
    def _():
        own_cols.start()

    pl.semaphore_wait(barrier, len(near))

    def remote(src, dst, send, recv, device):
        return pltpu.make_async_remote_copy(
            src_ref=src, dst_ref=dst, send_sem=send, recv_sem=recv, device_id=device, device_id_type=MESH
        )

    streams = []

    first, base = 0, 0
    u_lag0 = None
    for tree, count, stride in GROUPS:

        def u_part(ref, j, first=first):
            j = j + first
            col = pl.multiple_of(j // 2 * 128, 128)
            row = pl.multiple_of(lax.rem(j, 2) * 128, 128)
            return ref.at[pl.ds(row, 128), pl.ds(col, 128)]

        lag = base + lut(p, depths(tree))
        if u_lag0 is None:
            u_lag0 = lag
        children = []
        for slot in range(2):
            offs = offsets(tree, slot)
            if any(offs):
                off = lut(p, offs)
                children.append((off != 0, at_y(sign * off), lambda j, s=slot, f=first: (us.at[s, f + j], ur.at[f + j])))
        children.append((None, partner, lambda j, f=first: (ps.at[f + j], pr.at[f + j])))
        streams.append(
            dict(
                n=count,
                stride=stride,
                lag=lag,
                is_src=src_u,
                src=lambda j, part=u_part: part(mat, j),
                buf=lambda j, part=u_part: part(U.at[core], j),
                recv=lambda j, f=first: ur.at[f + j],
                children=children,
            )
        )
        first += count
        base += count * stride

    def plane(block):
        xr_ = lax.rem(x, NX) if block == 0 else lax.rem(1 - x + NX, NX)
        xs_ = 1 if block == 0 else -1
        lag = lut(z, depths(BOTH)) + lut(xr_, (0, HOP, 2 * HOP, HOP))
        children = []
        for slot in range(2):
            off = lut(z, offsets(BOTH, slot))
            children.append(((xr_ == 0) & (off != 0), at_z(off)))
        children.append((xr_ == 0, at_x(xs_)))
        off = lut(xr_, (-1, 0, 0, -1))
        children.append((off != 0, at_x(xs_ * off)))
        return lag, children, (xr_ == 0) & (z == 0)

    for block in range(2):
        lag, kids, is_src = plane(block)

        def l_part(ref, j):
            return ref.at[pl.ds(pl.multiple_of(j * LROWS, LROWS), LROWS), pl.ds(0, NB)]

        streams.append(
            dict(
                n=LCH,
                stride=2,
                lag=lag + block,
                is_src=is_src,
                src=lambda j: l_part(mat, j),
                buf=lambda j, b=block: l_part(L.at[b], j),
                recv=lambda j, b=block: lr.at[b, j],
                children=[
                    (cond, dev, lambda j, s=s, b=block: (ls.at[b, s, j], lr.at[b, j])) for s, (cond, dev) in enumerate(kids)
                ],
            )
        )

        mine = core == 1 - block
        x_lag = jnp.maximum(u_lag0 + 9, 2 * LCH) + lag
        streams.append(
            dict(
                n=XCH,
                stride=2,
                lag=x_lag,
                only=mine,
                is_src=is_src,
                src=lambda j: l_part(U.at[core], j),
                buf=lambda j: l_part(X.at[core], j),
                recv=lambda j: xr.at[j],
                children=[
                    (cond, dev, lambda j, s=s: (xs.at[s, j], xr.at[j])) for s, (cond, dev) in enumerate(kids)
                ]
                + [(None, partner, lambda j: (xp.at[j], xq.at[j]))],
            )
        )

    def when(cond, fn):
        if cond is None:
            fn()
        else:
            pl.when(cond)(fn)

    def handle(s, i):
        t = i - s["lag"]
        ok = (t >= 0) & (t < s["n"] * s["stride"])
        if s["stride"] > 1:
            ok = ok & (lax.rem(t, s["stride"]) == 0)
        if s.get("only") is not None:
            ok = ok & s["only"]

        @pl.when(ok)
        def _():
            j = t // s["stride"]

            def send(src):
                for cond, dev, sems in s["children"]:
                    a, b = sems(j)
                    when(cond, remote(src, s["buf"](j), a, b, dev).start)

            @pl.when(s["is_src"])
            def _():
                send(s["src"](j))

            @pl.when(jnp.logical_not(s["is_src"]))
            def _():
                buf = s["buf"](j)
                remote(buf, buf, s["recv"](j), s["recv"](j), partner).wait_recv()
                send(buf)

    steps = 160

    @pl.loop(0, steps)
    def _(i):
        @pl.when((i == 8) & src_u)
        def _():
            own_rows.wait()

        for s in streams:
            handle(s, i)

    @pl.when(src_l)
    def _():
        own_cols.wait()

    corner_src = src_l & (c == 1 - core)
    corner = pltpu.make_async_copy(U.at[core, :, pl.ds(0, NB)], X.at[core], loc.at[5])

    @pl.when(corner_src)
    def _():
        corner.start()
        corner.wait()

    @pl.loop(0, UCH)
    def _(j):
        col = pl.multiple_of(j // 2 * 128, 128)
        row = pl.multiple_of(lax.rem(j, 2) * 128, 128)
        buf = U.at[1 - core, pl.ds(row, 128), pl.ds(col, 128)]
        remote(buf, buf, pr.at[j], pr.at[j], partner).wait_recv()

    @pl.loop(0, XCH)
    def _(j):
        buf = X.at[1 - core, pl.ds(pl.multiple_of(j * LROWS, LROWS), LROWS)]
        remote(buf, buf, xq.at[j], xq.at[j], partner).wait_recv()

    for copy in local:
        copy.wait()

    li0h, li0l = split(inv[0, 0])
    li1h, li1l = split(inv[0, 1])
    ui0h, ui0l = split(inv[1, 0])
    ui1h, ui1l = split(inv[1, 1])
    for k, value in enumerate((li0h, li0l, li1h, li1l)):
        work[k] = value
    l10[...] = (dot(X[1], ui0h) + dot(X[1], ui0l)).astype(BF16)
    u01[...] = (dot(li0h, X[0]) + dot(li0l, X[0])).astype(BF16)
    for half in range(2):
        rows = pl.ds(half * NB, NB)
        block = half * 16 + r
        lower0 = dot(L[0, rows], ui0h) + dot(L[0, rows], ui0l)
        lower0 = jnp.where(block > 0, lower0, 0.0).astype(BF16)
        LF[rows, 0:NB] = lower0
        column = L[1, rows].astype(F32) - dot(lower0, u01[...])
        ch, cl = split(column)
        lower1 = dot(ch, ui1h) + dot(cl, ui1h) + dot(ch, ui1l)
        LF[rows, NB : 2 * NB] = jnp.where(block > 1, lower1, 0.0).astype(BF16)

    @pl.loop(0, 7)
    def _(q):
        cols = pl.ds(pl.multiple_of(q * NB, NB), NB)
        block = q * 32 + c
        upper0 = dot(work[0], U[0, :, cols]) + dot(work[1], U[0, :, cols])
        upper0 = jnp.where(block > 0, upper0, 0.0).astype(BF16)
        top = U[1, :, cols].astype(F32) - dot(l10[...], upper0)
        th, tl = split(top)
        upper1 = dot(work[2], th) + dot(work[3], th) + dot(work[2], tl)
        upper1 = jnp.where(block > 1, upper1, 0.0).astype(BF16)
        UF[0:NB] = upper0
        UF[NB : 2 * NB] = upper1
        out[:, cols] = (M[:, cols].astype(F32) - dot(LF[...], UF[...])).astype(BF16)

        @pl.when((r == 0) & (block > 0))
        def _():
            out[0:NB, cols] = UF[0:NB]

        @pl.when((r == 1) & (block > 1))
        def _():
            out[0:NB, cols] = UF[NB : 2 * NB]

    @pl.when((c == 0) & (r > 0))
    def _():
        out[0:NB, 0:NB] = LF[0:NB, 0:NB]

    @pl.when(c == 0)
    def _():
        out[NB : 2 * NB, 0:NB] = LF[NB : 2 * NB, 0:NB]

    @pl.when((c == 1) & (r > 1))
    def _():
        out[0:NB, 0:NB] = LF[0:NB, NB : 2 * NB]

    @pl.when(c == 1)
    def _():
        out[NB : 2 * NB, 0:NB] = LF[NB : 2 * NB, NB : 2 * NB]

    for s in streams:

        def drain(s=s):
            @pl.loop(0, s["n"])
            def _(j):
                for cond, dev, sems in s["children"]:
                    a, b = sems(j)
                    when(cond, remote(s["buf"](j), s["buf"](j), a, b, dev).wait_send)

        when(s.get("only"), drain)


def body(matrix, lower_inv, upper_inv):
    D = pltpu.SemaphoreType.DMA
    return pl.pallas_call(
        kernel,
        out_shape=jax.ShapeDtypeStruct(matrix.shape, matrix.dtype),
        in_specs=[pl.BlockSpec(memory_space=pl.ANY)] * 3,
        out_specs=pl.BlockSpec(memory_space=pltpu.VMEM),
        scratch_shapes=[
            pltpu.VMEM((2, NB, 1792), BF16),
            pltpu.VMEM((2, NB, NB), BF16),
            pltpu.VMEM((2, 512, NB), BF16),
            pltpu.VMEM((512, 1792), BF16),
            pltpu.VMEM((2, 2, NB, NB), F32),
            pltpu.VMEM((512, 512), BF16),
            pltpu.VMEM((512, NB), BF16),
            pltpu.VMEM((4, NB, NB), BF16),
            pltpu.VMEM((NB, NB), BF16),
            pltpu.VMEM((NB, NB), BF16),
            D((2, UCH)),
            D((UCH,)),
            D((UCH,)),
            D((UCH,)),
            D((2, 4, LCH)),
            D((2, LCH)),
            D((4, XCH)),
            D((XCH,)),
            D((XCH,)),
            D((XCH,)),
            D((6,)),
        ],
        compiler_params=pltpu.CompilerParams(
            collective_id=0, has_side_effects=True, vmem_limit_bytes=60 * 2**20
        ),
    )(matrix, lower_inv, upper_inv)


def solution(mesh):
    in_specs = (P("row", "col"), P(), P())
    return jax.shard_map(body, mesh=mesh, in_specs=in_specs, out_specs=P("row", "col"), check_vma=False)
```

time: 579 us -> 61.7 us (0.11)
  the two profiles are of different devices: /device:TPU:1 before, /device:TPU:60 now
where the time goes in v1:
time: 61.7 us; the launch traced here: 61.6 us
  Pallas kernels  58.7 us (95%)
  local copies, waits for them, and re-layouts  2.85 us (5%)
    pallas_call x1, Pallas kernels, body(): pl.pallas_call(kernel, out_shape=jax.ShapeDtypeStruct(matrix.shape, matri...  58.7 us
    unnamed x1, local copies, waits for them, and re-layouts  2.85 us

profile of v1, /device:TPU:60, one launch (start us, length us, event | category | flops | bytes accessed | tf_op | source)
XLA Modules:
  0.0 61.6 jit_solution(13430980763900926569)
XLA Ops:
  0.0 58.7 %shard_map.37 = bf16[512,1792]{1,0:T(8,128)(2,1)} custom-call(bf16[512,1792]{1,0:T(8,128)(2,1)} %mat.1, f32[2,256,256]{2,1,0:T(8,128)} %linv.1, f32[2,256,256]{2,1,0:T(8,128)} %uinv.1), custom_call_target="tpu_custom_call" | custom-call | tf_op jit(solution)/shard_map/pallas_call | solution.py:348
  58.7 2.8 %copy.5 = bf16[512,1792]{1,0:T(8,128)(2,1)} copy(bf16[512,1792]{1,0:T(8,128)(2,1)} %shard_map.37) | data formatting | bytes 3670016

commit v2 on v0

v2 whole, which is shorter than its diff:
```python
import jax
import jax.numpy as jnp
from jax import lax
from jax.experimental import pallas as pl
from jax.experimental.pallas import tpu as pltpu
from jax.sharding import PartitionSpec as P

MESH = pl.DeviceIdType.MESH
F32 = jnp.float32
BF16 = jnp.bfloat16
NB = 256
COLS = 1792
NY, NZ, NX = 8, 8, 4

NEAR = {0: (1, 7), 1: (2,), 2: (3,), 3: (4,), 7: (6,), 6: (5,)}
FAR = {0: (2, 6), 2: (1, 3), 3: (4,), 6: (7, 5)}
WIDE = {0: (2, 6), 2: (4, 3, 1), 6: (5, 7)}
LONG = {0: (2,), 2: (3, 1), 3: (4,), 4: (5,), 5: (6,), 6: (7,)}

GROUPS = (
    (WIDE, 0, 4, 0, 1, (0, 9, 5, 9, 10, 8, 5, 8)),
    (LONG, 4, 16, 4, 2, (-4, 9, 5, 9, 13, 17, 21, 25)),
    (NEAR, 20, 8, 12, 1, (-2, 5, 8, 12, 16, 12, 8, 5)),
)
UCH = 28
LROWS = 64
LCH = 512 // LROWS
XCH = NB // LROWS
STEPS = 42
PLANE = (2, 9, 6, 9, 14, 9, 6, 9)
PLANE_X = (0, 9, 5, 9, 10, 8, 5, 8)


def offsets(tree, slot):
    out = []
    for k in range(8):
        children = tree.get(k, ())
        out.append((children[slot] - k + 4) % 8 - 4 if slot < len(children) else 0)
    return out


def lut(index, values):
    result = jnp.int32(values[0])
    for k in range(1, len(values)):
        if values[k] != values[0]:
            result = jnp.where(index == k, jnp.int32(values[k]), result)
    return result


def split(value):
    high = value.astype(BF16)
    return high, (value - high.astype(F32)).astype(BF16)


def dot(a, b):
    return jnp.dot(a, b, preferred_element_type=F32)


def remote(src, dst, send, recv, device):
    return pltpu.make_async_remote_copy(
        src_ref=src, dst_ref=dst, send_sem=send, recv_sem=recv, device_id=device, device_id_type=MESH
    )


def gather(mat, linv, uinv, UF, LF, M, U, X, L, inv, W, small, D1, us, ur, ps, pr, ls, lr, xs, xr, xp, xq, ready, loc):
    r = lax.axis_index("row")
    c = lax.axis_index("col")
    y, core = r // 2, lax.rem(r, 2)
    z, x = c // NX, lax.rem(c, NX)
    sign = 1 - 2 * core
    p = lax.rem(NY + sign * y, NY)
    partner = (y * 2 + 1 - core, c)
    hub = x < 2
    fb = jnp.where((x == 1) | (x == 2), 1, 0)
    xb = 1 - core
    src_u = p == 0
    src_l = c < 2
    src_x = c == xb

    def at_y(off):
        return (lax.rem(y + off + NY, NY) * 2 + core, c)

    def at_z(off):
        return (r, lax.rem(z + off + NZ, NZ) * NX + x)

    def at_x(off):
        return (r, z * NX + lax.rem(x + off + NX, NX))

    barrier = pltpu.get_barrier_semaphore()

    def greet(device):
        pl.semaphore_signal(barrier, inc=1, device_id=device, device_id_type=MESH)

    for device in (at_y(1), at_y(-1), at_y(2), at_y(-2), at_x(1), at_x(-1), at_x(2), partner):
        greet(device)
    z_links = lambda k: [(k, child) for child in sorted(set(FAR.get(k, ())) | set(WIDE.get(k, ())))]
    down = [[child - k for _, child in z_links(k)] for k in range(NZ)]
    up = [[parent - k for parent in range(NZ) if (parent, k) in z_links(parent)] for k in range(NZ)]
    most_down, most_up = max(map(len, down)), max(map(len, up))
    z_down = [lut(z, [(d[i] + 4) % 8 - 4 if i < len(d) else 0 for d in down]) for i in range(most_down)]
    z_up = [lut(z, [(d[i] + 4) % 8 - 4 if i < len(d) else 0 for d in up]) for i in range(most_up)]
    n_down = lut(z, [len(d) for d in down])
    n_up = lut(z, [len(d) for d in up])
    for off in z_down:
        pl.when(hub & (off != 0))(lambda off=off: greet(at_z(off)))

    local = [
        pltpu.make_async_copy(linv, inv.at[0], loc.at[1]),
        pltpu.make_async_copy(uinv, inv.at[1], loc.at[2]),
        pltpu.make_async_copy(mat, M, loc.at[0]),
    ]
    own_rows = pltpu.make_async_copy(mat.at[pl.ds(0, NB)], U.at[core], loc.at[3])
    own_cols = pltpu.make_async_copy(mat.at[:, pl.ds(0, NB)], L.at[fb], loc.at[4])
    local[0].start()
    local[1].start()
    pl.when(src_u)(own_rows.start)
    pl.when(src_l)(own_cols.start)
    local[2].start()
    local[0].wait()
    local[1].wait()
    for k in range(4):
        high, low = split(inv[k // 2, k % 2])
        W[k, 0] = high
        W[k, 1] = low
    pl.when(src_u)(own_rows.wait)
    pl.when(src_l)(own_cols.wait)
    local[2].wait()
    pl.semaphore_wait(barrier, 8 + jnp.where(hub, n_up, 0))
    for off in z_up:

        @pl.when(hub & (off != 0))
        def _(off=off):
            pl.semaphore_signal(ready, inc=1, device_id=at_z(off), device_id_type=MESH)

    def u_part(ref, j):
        col = pl.multiple_of(j // 2 * 128, 128)
        row = pl.multiple_of(lax.rem(j, 2) * 128, 128)
        return ref.at[pl.ds(row, 128), pl.ds(col, 128)]

    def u_children(tree):
        out = []
        for slot in range(3):
            offs = offsets(tree, slot)
            if any(offs):
                off = lut(p, offs)
                out.append((slot, off != 0, at_y(sign * off)))
        return out

    def half(side):
        return pl.ds(pl.multiple_of(side * NB, NB), NB)

    def panel(q):
        cols = pl.ds(pl.multiple_of(q * NB, NB), NB)
        raw = U[core, :, cols]
        value = dot(W[core, 0], raw) + dot(W[core, 1], raw)
        UF[half(core), cols] = jnp.where((q > 0) | (c > 1), value, 0.0).astype(BF16)
        mine = UF.at[half(core), cols]
        remote(mine, mine, ps.at[0], pr.at[0], partner).start()

        @pl.when((r == 0) & ((q > 0) | (c > 0)))
        def _():
            M[0:NB, cols] = value.astype(BF16)

    sequences = []
    for g, (tree, first, count, start, rate, arrival) in enumerate(GROUPS):

        def own(j, g=g, first=first, tree=tree):
            j = j + first
            buf = u_part(U.at[core], j)

            @pl.when(jnp.logical_not(src_u))
            def _():
                remote(buf, buf, ur.at[j], ur.at[j], partner).wait_recv()

            for slot, cond, device in u_children(tree):
                pl.when(cond)(remote(buf, buf, us.at[g, slot], ur.at[j], device).start)

            @pl.when(lax.rem(j, 4) == 3)
            def _():
                panel(j // 4)

        sequences.append((start + lut(p, arrival), rate, count, own))

    def rows_of(j):
        return pl.ds(pl.multiple_of(j * LROWS, LROWS), LROWS)

    plane = []
    for slot in range(2):
        off = lut(z, offsets(FAR, slot))
        plane.append((hub & (off != 0), at_z(off)))
    plane.append((hub, at_x(1)))
    plane.append((hub | (x == 3), at_x(-1)))
    plane.append((x == 2, at_x(1)))
    plane_x = []
    for slot in range(3):
        off = lut(z, offsets(WIDE, slot))
        plane_x.append((off != 0, at_z(off)))
    plane_x += [(None, at_x(2)), (None, at_x(1)), (None, at_x(-1))]

    def when(cond, fn):
        if cond is None:
            fn()
        else:
            pl.when(cond)(fn)

    def from_hub(block):
        return jnp.where(block == 0, x, lax.rem(1 - x + NX, NX))

    def column(j):
        buf = L.at[fb, rows_of(j)]

        @pl.when(hub & (n_down > 0) & (j == 0))
        def _():
            pl.semaphore_wait(ready, n_down)

        @pl.when(jnp.logical_not(src_l))
        def _():
            remote(buf, buf, lr.at[fb, j], lr.at[fb, j], partner).wait_recv()

        for slot, (cond, device) in enumerate(plane):
            pl.when(cond)(remote(buf, buf, ls.at[slot], lr.at[fb, j], device).start)

    def corner(j):
        buf = X.at[core, rows_of(j)]

        @pl.when(src_x)
        def _():
            X[core, rows_of(j)] = U[core, rows_of(j), 0:NB]

        @pl.when(jnp.logical_not(src_x))
        def _():
            remote(buf, buf, xr.at[j], xr.at[j], partner).wait_recv()

        @pl.when(x == xb)
        def _():
            for slot, (cond, device) in enumerate(plane_x):
                when(cond, remote(buf, buf, xs.at[slot], xr.at[j], device).start)

        remote(buf, buf, xp.at[0], xq.at[0], partner).start()

    def lower(_):
        @pl.loop(0, LCH)
        def _(j):
            buf = L.at[1 - fb, rows_of(j)]
            remote(buf, buf, lr.at[1 - fb, j], lr.at[1 - fb, j], partner).wait_recv()

        for part in range(2):
            rows = pl.ds(part * NB, NB)
            raw0, raw1 = L[0, rows], L[1, rows]
            lower0 = dot(raw0, W[2, 0]) + dot(raw0, W[2, 1])
            LF[rows, 0:NB] = jnp.where(part * 16 + r > 0, lower0, 0.0).astype(BF16)
            D1[rows] = dot(raw1, W[3, 0]) + dot(raw1, W[3, 1])

    def corners(_):
        buf = X.at[1 - core]
        remote(buf, buf, xq.at[0], xq.at[0], partner).wait_recv()
        l10 = (dot(X[1], W[2, 0]) + dot(X[1], W[2, 1])).astype(BF16)
        u01 = (dot(W[0, 0], X[0]) + dot(W[0, 1], X[0])).astype(BF16)
        small[0] = (dot(W[1, 0], l10) + dot(W[1, 1], l10)).astype(BF16)
        small[1] = (dot(u01, W[3, 0]) + dot(u01, W[3, 1])).astype(BF16)
        small[2] = u01
        for part in range(2):
            rows = pl.ds(part * NB, NB)
            block = part * 16 + r
            lower0 = LF[rows, 0:NB]
            lower1 = D1[rows] - dot(lower0, small[1])
            lower1 = jnp.where(block > 1, lower1, 0.0).astype(BF16)

            @pl.when((c == 0) & (block > 0))
            def _():
                M[rows, 0:NB] = lower0

            @pl.when((c == 1) & (block > 1))
            def _():
                M[rows, 0:NB] = lower1

            if part == 0:

                @pl.when((c == 1) & (r == 1))
                def _():
                    M[rows, 0:NB] = (M[rows, 0:NB].astype(F32) - dot(lower0, small[2])).astype(BF16)

            LF[rows, 0:NB] = (lower0.astype(F32) - dot(lower1, small[0])).astype(BF16)
            LF[rows, NB : 2 * NB] = lower1

    from_z = lut(z, PLANE)
    from_x = jnp.maximum(lut(from_hub(0), (0, 5, 10, 6)), lut(from_hub(1), (0, 5, 10, 6)))
    sequences.append((from_z + lut(from_hub(fb), (0, 5, 10, 6)), 1, LCH, column))
    x_ready = jnp.maximum(LCH, 5 + lut(p, GROUPS[0][5])) + lut(z, PLANE_X)
    sequences.append((x_ready + lut(from_hub(xb), (0, 6, 7, 6)), 1, XCH, corner))
    sequences.append((from_z + from_x + LCH + 4, 1, 1, lower))
    sequences.append((jnp.maximum(from_z + from_x + LCH + 4, x_ready + 7 + XCH + 4), 1, 1, corners))

    def step(it, done):
        now = []
        for (start, rate, count, handle), begin in zip(sequences, done):
            end = jnp.clip((it + 1 - start) * rate, 0, count)
            end = jnp.where(it == STEPS - 1, count, end)
            lax.fori_loop(begin, end, lambda j, _, handle=handle: (handle(j), jnp.int32(0))[1], jnp.int32(0))
            now.append(end)
        return tuple(now)

    lax.fori_loop(0, STEPS, step, tuple(jnp.int32(0) for _ in sequences))

    theirs = UF.at[half(1 - core)]
    remote(theirs, theirs, pr.at[0], pr.at[0], partner).wait_recv()

    @pl.when(r == 1)
    def _():
        LF[0:NB] = jnp.zeros((NB, 2 * NB), BF16)

        @pl.loop(0, COLS // NB)
        def _(q):
            cols = pl.ds(pl.multiple_of(q * NB, NB), NB)
            raw = U[1, :, cols]

            @pl.when((q > 0) | (c > 1))
            def _():
                value = dot(W[1, 0], raw) + dot(W[1, 1], raw) - dot(small[0], UF[0:NB, cols])
                M[0:NB, cols] = value.astype(BF16)

    for g, (tree, first, count, _, _, _) in enumerate(GROUPS):
        buf = U.at[core, :, pl.ds(first * 64, count * 64)]
        for slot, cond, device in u_children(tree):
            pl.when(cond)(remote(buf, buf, us.at[g, slot], ur.at[0], device).wait_send)
    remote(theirs, theirs, ps.at[0], pr.at[0], partner).wait_send()
    for slot, (cond, device) in enumerate(plane):
        pl.when(cond)(remote(L.at[fb], L.at[fb], ls.at[slot], lr.at[fb, 0], device).wait_send)

    @pl.when(x == xb)
    def _():
        for slot, (cond, device) in enumerate(plane_x):
            when(cond, remote(X.at[core], X.at[core], xs.at[slot], xr.at[0], device).wait_send)

    remote(X.at[core], X.at[core], xp.at[0], xq.at[0], partner).wait_send()


def update(UF, LF, M, out, O, sems):
    copies = []
    for q in range(COLS // NB):
        cols = pl.ds(q * NB, NB)
        O[:, cols] = (M[:, cols].astype(F32) - dot(LF[...], UF[:, cols])).astype(BF16)
        copies.append(pltpu.make_async_copy(O.at[:, cols], out.at[:, cols], sems.at[q]))
        copies[-1].start()
    for copy in copies:
        copy.wait()


def body(matrix, lower_inv, upper_inv):
    D = pltpu.SemaphoreType.DMA
    vmem = pl.BlockSpec(memory_space=pltpu.VMEM)
    hbm = pl.BlockSpec(memory_space=pltpu.HBM)
    UF, LF, M = pl.pallas_call(
        gather,
        out_shape=(
            jax.ShapeDtypeStruct((2 * NB, COLS), BF16),
            jax.ShapeDtypeStruct((512, 2 * NB), BF16),
            jax.ShapeDtypeStruct((512, COLS), BF16),
        ),
        in_specs=[hbm] * 3,
        out_specs=(vmem, vmem, vmem),
        scratch_shapes=[
            pltpu.VMEM((2, NB, COLS), BF16),
            pltpu.VMEM((2, NB, NB), BF16),
            pltpu.VMEM((2, 512, NB), BF16),
            pltpu.VMEM((2, 2, NB, NB), F32),
            pltpu.VMEM((4, 2, NB, NB), BF16),
            pltpu.VMEM((3, NB, NB), BF16),
            pltpu.VMEM((512, NB), F32),
            D((3, 3)),
            D((UCH,)),
            D((1,)),
            D((1,)),
            D((5,)),
            D((2, LCH)),
            D((6,)),
            D((XCH,)),
            D((1,)),
            D((1,)),
            pltpu.SemaphoreType.REGULAR,
            D((5,)),
        ],
        compiler_params=pltpu.CompilerParams(
            collective_id=0, has_side_effects=True, vmem_limit_bytes=32 * 2**20
        ),
    )(*(pltpu.with_memory_space_constraint(a, pltpu.HBM) for a in (matrix, lower_inv, upper_inv)))
    return pl.pallas_call(
        update,
        out_shape=jax.ShapeDtypeStruct(matrix.shape, matrix.dtype),
        in_specs=[vmem] * 3,
        out_specs=hbm,
        scratch_shapes=[pltpu.VMEM((512, COLS), BF16), D((COLS // NB,))],
        compiler_params=pltpu.CompilerParams(vmem_limit_bytes=16 * 2**20),
    )(UF, LF, M)


def solution(mesh):
    in_specs = (P("row", "col"), P(), P())
    return jax.shard_map(body, mesh=mesh, in_specs=in_specs, out_specs=P("row", "col"), check_vma=False)
```

time: 579 us -> 44.4 us (0.08)
  the two profiles are of different devices: /device:TPU:1 before, /device:TPU:120 now
where the time goes in v2:
time: 44.4 us; the launch traced here: 44.3 us
  Pallas kernels  44.3 us (100%)
    pallas_call x1, Pallas kernels, body(): pl.pallas_call(gather, out_shape=(jax.ShapeDtypeStruct((2 * NB, COLS), BF...  42.3 us
    pallas_call x1, Pallas kernels, body(): pl.pallas_call(update, out_shape=jax.ShapeDtypeStruct(matrix.shape, matri...  2.02 us

profile of v2, /device:TPU:120, one launch (start us, length us, event | category | flops | bytes accessed | tf_op | source)
XLA Modules:
  0.0 44.3 jit_solution(5410702734778403970)
XLA Ops:
  0.0 42.3 %shard_map.37 = (bf16[512,1792]{1,0:T(8,128)(2,1)S(1)}, bf16[512,512]{1,0:T(8,128)(2,1)S(1)}, bf16[512,1792]{1,0:T(8,128)(2,1)S(1)}) custom-call(bf16[512,1792]{1,0:T(8,128)(2,1)} %mat.1, f32[2,256,256]{2,1,0:T(8,128)} %linv.1, f32[2,256,256]{2,1,0:T(8,128)} %uinv.1), custom_call_target="tpu_custom_call" | custom-call | tf_op jit(solution)/shard_map/pallas_call | solution.py:353
  42.3 2.0 %shard_map.38 = bf16[512,1792]{1,0:T(8,128)(2,1)} custom-call(bf16[512,1792]{1,0:T(8,128)(2,1)S(1)} %get-tuple-element.8.UF, bf16[512,512]{1,0:T(8,128)(2,1)S(1)} %get-tuple-element.9.LF, bf16[512,1792]{1,0:T(8,128)(2,1)S(1)} %get-tuple-element.10.M), custom_call_target="tpu_custom_call" | custom-call | tf_op jit(solution)/shard_map/pallas_call | solution.py:387

commit v3 on v2

v3 whole, which is shorter than its diff:
```python
import jax
import jax.numpy as jnp
from jax import lax
from jax.experimental import pallas as pl
from jax.experimental.pallas import tpu as pltpu
from jax.sharding import PartitionSpec as P

MESH = pl.DeviceIdType.MESH
F32 = jnp.float32
BF16 = jnp.bfloat16
NB = 256
COLS = 1792
NY, NZ, NX = 8, 8, 4

NEAR = {0: (1, 7), 1: (2,), 2: (3,), 3: (4,), 7: (6,), 6: (5,)}
FAR = {0: (2, 6), 2: (1, 3), 3: (4,), 6: (7, 5)}
WIDE = {0: (2, 6), 2: (4, 3, 1), 6: (5, 7)}
LONG = {0: (2,), 2: (3, 1), 3: (4,), 4: (5,), 5: (6,), 6: (7,)}

GROUPS = (
    (FAR, 0, 4, 0, 1, (0, 8, 5, 8, 11, 8, 5, 8)),
    (LONG, 4, 16, 4, 2, (-4, 8, 4, 8, 11, 15, 18, 21)),
    (NEAR, 20, 8, 12, 1, (-8, 4, 7, 10, 14, 10, 7, 4)),
)
UCH = 28
SHARED = 5
LROWS = 64
LCH = 1024 // LROWS
XCH = NB // LROWS
STEPS = 36
LOWER_AT = 30
PLANE = (0, 10, 6, 10, 15, 10, 6, 10)
FROM_HUB = (0, 5, 10, 6)
PLANE_X = (0, 10, 6, 10, 11, 9, 6, 9)


def offsets(tree, slot):
    out = []
    for k in range(8):
        children = tree.get(k, ())
        out.append((children[slot] - k + 4) % 8 - 4 if slot < len(children) else 0)
    return out


def lut(index, values):
    result = jnp.int32(values[0])
    for k in range(1, len(values)):
        if values[k] != values[0]:
            result = jnp.where(index == k, jnp.int32(values[k]), result)
    return result


def split(value):
    high = value.astype(BF16)
    return high, (value - high.astype(F32)).astype(BF16)


def dot(a, b):
    return jnp.dot(a, b, preferred_element_type=F32)


def remote(src, dst, send, recv, device):
    return pltpu.make_async_remote_copy(
        src_ref=src, dst_ref=dst, send_sem=send, recv_sem=recv, device_id=device, device_id_type=MESH
    )


def gather(
    mat, linv, uinv, UF, LF, M, U, X, L, inv, W, small, D1, us, ur, ps, pr, fs, fr, ls, lr, ll, lq, xs, xr, xl, xq, B1, ready, loc
):
    r = lax.axis_index("row")
    c = lax.axis_index("col")
    y, core = r // 2, lax.rem(r, 2)
    z, x = c // NX, lax.rem(c, NX)
    partner = (y * 2 + 1 - core, c)
    first_core = core == 0
    hub = x < 2
    fb = jnp.where((x == 1) | (x == 2), 1, 0)
    hb = jnp.where(x == 0, 1, 0)
    turn = jnp.where(lax.rem(x, 2) == 0, 1, -1)
    src_l = c < 2

    def at_y(off, to_core):
        return (lax.rem(y + off + NY, NY) * 2 + to_core, c)

    def at_z(off):
        return (r, lax.rem(z + off + NZ, NZ) * NX + x)

    def at_x(off, to_core):
        return (y * 2 + to_core, z * NX + lax.rem(x + off + NX, NX))

    def u_part(ref, j):
        col = pl.multiple_of(j // 2 * 128, 128)
        row = pl.multiple_of(lax.rem(j, 2) * 128, 128)
        return ref.at[pl.ds(row, 128), pl.ds(col, 128)]

    def block(q):
        return pl.ds(pl.multiple_of(q * NB, NB), NB)

    barrier = pltpu.get_barrier_semaphore()

    def greet(device):
        pl.semaphore_signal(barrier, inc=1, device_id=device, device_id_type=MESH)

    z_links = [(k, child) for k in range(NZ) for child in sorted(set(FAR.get(k, ())) | set(WIDE.get(k, ())))]
    down = [[child - k for k, child in z_links if k == at] for at in range(NZ)]
    up = [[k - child for k, child in z_links if child == at] for at in range(NZ)]
    z_down = [lut(z, [(d[i] + 4) % 8 - 4 if i < len(d) else 0 for d in down]) for i in range(max(map(len, down)))]
    z_up = [lut(z, [(d[i] + 4) % 8 - 4 if i < len(d) else 0 for d in up]) for i in range(max(map(len, up)))]
    n_down = lut(z, [len(d) for d in down])
    n_up = lut(z, [len(d) for d in up])
    rank = [[down[(at + off) % NZ].index(-off) for off in d] for at, d in enumerate(up)]
    z_rank = [lut(z, [k[i] if i < len(k) else 0 for k in rank]) for i in range(len(z_up))]

    greet(partner)
    greet(at_x(turn, 0))

    @pl.when(first_core)
    def _():
        pl.when(x != 0)(lambda: greet(at_x(-x, 0)))
        pl.when(x != 1)(lambda: greet(at_x(1 - x, 0)))
        pl.when(x >= 2)(lambda: greet(at_x(-turn, 0)))
        for off in z_down:
            pl.when(hub & (off != 0))(lambda off=off: greet(at_z(off)))

    @pl.when(core == 1)
    def _():
        for off in (1, -1, 2, -2):
            greet(at_y(off, 1))
        pl.when((y == 1) | (y == 2) | (y == 6) | (y == 7))(lambda: greet((0, c)))

    local = [
        pltpu.make_async_copy(linv, inv.at[0], loc.at[1]),
        pltpu.make_async_copy(uinv, inv.at[1], loc.at[2]),
        pltpu.make_async_copy(mat, M, loc.at[0]),
    ]
    mine = pl.ds(pl.multiple_of(core * 512, 512), 512)
    own_rows = pltpu.make_async_copy(mat.at[pl.ds(0, NB)], U.at[core], loc.at[3])
    own_cols = pltpu.make_async_copy(mat.at[:, pl.ds(0, NB)], L.at[mine], loc.at[4])
    local[0].start()
    local[1].start()
    pl.when(y == 0)(own_rows.start)
    pl.when(src_l)(own_cols.start)
    local[2].start()
    count_0 = 3 + jnp.where(hub, 4 + n_up, 0) + jnp.where(y == 0, 4, 0)
    pl.semaphore_wait(barrier, jnp.where(first_core, count_0, 5))

    @pl.when(y == 0)
    def _():
        for side in range(2):

            @pl.when(core == side)
            def _(side=side):
                for g, (tree, first, count, _, _, _) in enumerate(GROUPS):

                    @pl.loop(first, first + count)
                    def _(j, g=g, tree=tree):
                        for slot, child in enumerate(tree[0]):
                            off = child if child <= 4 else child - 8
                            remote(
                                u_part(mat, j),
                                u_part(U.at[side], j),
                                us.at[side, g, slot],
                                ur.at[side, j],
                                at_y(off if side == 0 else -off, 1),
                            ).start()

                if side == 1:

                    @pl.loop(0, 7)
                    def _(q):
                        raw = mat.at[pl.ds(0, NB), block(q)]
                        remote(raw, U.at[1, :, block(q)], ps.at[1], pr.at[1, q], partner).start()

                else:
                    remote(mat.at[pl.ds(0, NB)], U.at[0], ps.at[0], pr.at[0, 0], partner).start()

    for off, place in zip(z_up, z_rank):

        @pl.when(first_core & hub & (off != 0))
        def _(off=off, place=place):
            pl.semaphore_signal(ready.at[place], inc=1, device_id=at_z(off), device_id_type=MESH)

    local[0].wait()
    local[1].wait()
    for k in range(4):
        high, low = split(inv[k // 2, k % 2])
        W[k, 0] = high
        W[k, 1] = low
    pl.when(y == 0)(own_rows.wait)
    pl.when(src_l)(own_cols.wait)
    local[2].wait()

    positions = (y, lax.rem(NY - y, NY))

    def u_children(side, tree):
        out = []
        for slot in range(2):
            offs = offsets(tree, slot)
            if any(offs):
                off = lut(positions[side], offs)
                out.append((slot, off != 0, at_y(off if side == 0 else -off, 1)))
        return out

    def panel(side, q):
        cols = block(q)
        raw = U[side, :, cols]
        value = dot(W[side, 0], raw) + dot(W[side, 1], raw)
        UF[block(side), cols] = jnp.where((q > 0) | (c > 1), value, 0.0).astype(BF16)

        @pl.when((r == 0) & (side == 0) & ((q > 0) | (c > 0)))
        def _():
            M[0:NB, cols] = value.astype(BF16)

    def hand_on(side, g, first, tree):
        def event(j):
            j = j + first
            buf = u_part(U.at[side], j)
            remote(buf, buf, ur.at[side, j], ur.at[side, j], partner).wait_recv()
            for slot, cond, device in u_children(side, tree):
                pl.when(cond)(remote(buf, buf, us.at[side, g, slot], ur.at[side, j], device).start)

            @pl.when(lax.rem(j, 4) == 3)
            def _():
                q = j // 4
                raw = U.at[side, :, block(q)]
                remote(raw, raw, ps.at[side], pr.at[side, q], partner).start()
                if first >= 4 * SHARED:
                    panel(side, q)

        return event

    def take(side, q):
        @pl.when((y != 0) | (side == 1))
        def _():
            raw = U.at[side, :, block(q)]
            remote(raw, raw, pr.at[side, q], pr.at[side, q], partner).wait_recv()

        panel(side, q)

    def take_and_give(side, q):
        take(side, q)
        done = UF.at[block(side), block(q)]
        remote(done, done, fs.at[0], fr.at[0], partner).start()

    on_1 = []
    for side in range(2):
        for g, (tree, first, count, start, rate, arrival) in enumerate(GROUPS):
            on_1.append((start + lut(positions[side], arrival), rate, count // rate, hand_on(side, g, first, tree)))

    def rows_of(j, base=0):
        return pl.ds(pl.multiple_of(base + j * LROWS, LROWS), LROWS)

    plane = []
    for slot in range(2):
        off = lut(z, offsets(FAR, slot))
        plane.append((hub & (off != 0), at_z(off)))
    plane.append((hub, at_x(-turn, 0)))
    plane_x = []
    for slot in range(3):
        off = lut(z, offsets(WIDE, slot))
        plane_x.append((off != 0, at_z(off)))

    def from_hub(side):
        return jnp.where(side == 0, x, lax.rem(1 - x + NX, NX))

    def column(j, slots):
        buf = L.at[rows_of(j)]

        @pl.when(jnp.logical_not(src_l))
        def _():
            remote(buf, buf, lr.at[j], lr.at[j], partner).wait_recv()

        for slot, (cond, device) in enumerate(plane):
            if slot in slots:
                pl.when(cond)(remote(buf, buf, ls.at[slot], lr.at[j], device).start)
        if 3 in slots:
            kept = L.at[rows_of(lax.rem(j, LCH // 2), 1024)]
            remote(buf, kept, ls.at[3], ll.at[0], at_x(turn, j // (LCH // 2))).start()

            @pl.when(jnp.logical_not(src_l) & (j >= LCH // 2))
            def _():
                remote(buf, buf, ls.at[4], lq.at[0], partner).start()

    def answered(place):
        @pl.when(hub & (n_down > place))
        def _():
            pl.semaphore_wait(ready.at[place], 1)

    def columns():
        @pl.when(src_l)
        def _():
            pl.loop(0, LCH // 2)(lambda j: column(j, (2, 3)))
            theirs = L.at[pl.ds(512, 512)]
            remote(theirs, theirs, lq.at[0], lq.at[0], partner).wait_recv()
            pl.loop(LCH // 2, LCH)(lambda j: column(j, (2, 3)))
            for slot in range(2):
                answered(slot)
                pl.loop(0, LCH)(lambda j: column(j, (slot,)))

        @pl.when(jnp.logical_not(src_l))
        def _():
            for place in range(3):
                answered(place)
            pl.loop(0, LCH)(lambda j: column(j, (0, 1, 2, 3)))

    def corner(j):
        buf = X.at[hb, rows_of(j)]

        @pl.when(z == 0)
        def _():
            X[hb, rows_of(j)] = U[hb, rows_of(j), 0:NB]

        @pl.when(z != 0)
        def _():
            remote(buf, buf, xr.at[j], xr.at[j], partner).wait_recv()

        for slot, (cond, device) in enumerate(plane_x):
            pl.when(cond)(remote(buf, buf, xs.at[slot], xr.at[j], device).start)
        for slot, off in enumerate((2, 1, -1)):
            remote(buf, buf, xs.at[3 + slot], xl.at[hb], at_x(off, 0)).start()

    def lower_rows(which, base):
        @pl.when(which == 0)
        def _():
            for part in range(2):
                raw = L[pl.ds(pl.multiple_of(base + part * NB, NB), NB)]
                value = dot(raw, W[2, 0]) + dot(raw, W[2, 1])
                LF[part * NB : (part + 1) * NB, 0:NB] = jnp.where(part * 16 + r > 0, value, 0.0).astype(BF16)

        @pl.when(which == 1)
        def _():
            for part in range(2):
                raw = L[pl.ds(pl.multiple_of(base + part * NB, NB), NB)]
                D1[part * NB : (part + 1) * NB] = dot(raw, W[3, 0]) + dot(raw, W[3, 1])

    def lower():
        @pl.when((core == 1) & jnp.logical_not(src_l))
        def _():
            remote(L.at[mine], L.at[mine], lq.at[0], lq.at[0], partner).wait_recv()

        lower_rows(fb, core * 512)
        kept = L.at[pl.ds(1024, 512)]
        remote(kept, kept, ll.at[0], ll.at[0], partner).wait_recv()
        lower_rows(1 - fb, 1024)

    def corners():
        @pl.when(first_core)
        def _():
            for k in range(2):

                @pl.when(x != 1 - k)
                def _():
                    remote(X.at[k], X.at[k], xl.at[k], xl.at[k], partner).wait_recv()

            remote(X, X, xs.at[6], xq.at[0], partner).start()

        @pl.when(core == 1)
        def _():
            remote(X, X, xq.at[0], xq.at[0], partner).wait_recv()

        l10 = (dot(X[1], W[2, 0]) + dot(X[1], W[2, 1])).astype(BF16)
        u01 = (dot(W[0, 0], X[0]) + dot(W[0, 1], X[0])).astype(BF16)
        small[0] = (dot(W[1, 0], l10) + dot(W[1, 1], l10)).astype(BF16)
        small[1] = (dot(u01, W[3, 0]) + dot(u01, W[3, 1])).astype(BF16)
        small[2] = u01
        for part in range(2):
            rows = pl.ds(part * NB, NB)
            at = part * 16 + r
            lower0 = LF[rows, 0:NB]
            lower1 = D1[rows] - dot(lower0, small[1])
            lower1 = jnp.where(at > 1, lower1, 0.0).astype(BF16)

            @pl.when((c == 0) & (at > 0))
            def _():
                M[rows, 0:NB] = lower0

            @pl.when((c == 1) & (at > 1))
            def _():
                M[rows, 0:NB] = lower1

            if part == 0:

                @pl.when((c == 1) & (r == 1))
                def _():
                    M[rows, 0:NB] = (M[rows, 0:NB].astype(F32) - dot(lower0, small[2])).astype(BF16)

            LF[rows, 0:NB] = (lower0.astype(F32) - dot(lower1, small[0])).astype(BF16)
            LF[rows, NB : 2 * NB] = lower1

    def steps(begin, end):
        @pl.loop(begin, end)
        def _(it):
            for start, rate, count, handle in on_1:
                k = it - start

                @pl.when((k >= 0) & (k < count))
                def _(k=k, rate=rate, handle=handle):
                    for i in range(rate):
                        handle(k * rate + i)

    @pl.when(first_core)
    def _():
        early = (y == 0) & (z != 0)
        near_side = jnp.where(y <= 4, 0, 1)

        def first_blocks():
            take_and_give(0, 0)
            take_and_give(1, 0)

        def near_blocks():
            pl.loop(1, SHARED)(lambda q: take_and_give(near_side, q))

        def far_blocks():
            @pl.loop(SHARED, 7)
            def _(q):
                take(0, q)
                take(1, q)

            pl.loop(1, SHARED)(lambda q: take_and_give(1 - near_side, q))

        @pl.when(early)
        def _():
            first_blocks()
            near_blocks()
            far_blocks()

        columns()
        pl.when(jnp.logical_not(early))(first_blocks)

        @pl.when(hub)
        def _():
            pl.loop(0, XCH)(corner)

        lower()
        pl.when(jnp.logical_not(early))(near_blocks)
        corners()
        pl.when(jnp.logical_not(early))(far_blocks)

        for g, (tree, first, count, _, _, _) in enumerate(GROUPS):
            buf = U.at[0, :, pl.ds(first * 64, count * 64)]
            for slot, cond, device in u_children(0, tree):
                pl.when(cond & (y == 0))(remote(buf, buf, us.at[0, g, slot], ur.at[0, 0], device).wait_send)
        pl.when(y == 0)(remote(U.at[0], U.at[0], ps.at[0], pr.at[0, 0], partner).wait_send)
        shared = UF.at[:, pl.ds(0, SHARED * NB)]
        remote(shared, shared, fs.at[0], fr.at[0], partner).wait_send()
        whole = L.at[pl.ds(0, 1024)]
        for slot, (cond, device) in enumerate(plane):
            pl.when(cond)(remote(whole, whole, ls.at[slot], lr.at[0], device).wait_send)
        remote(whole, whole, ls.at[3], ll.at[0], partner).wait_send()
        part = L.at[pl.ds(512, 512)]
        pl.when(jnp.logical_not(src_l))(remote(part, part, ls.at[4], lq.at[0], partner).wait_send)

        @pl.when(hub)
        def _():
            for slot, (cond, device) in enumerate(plane_x):
                pl.when(cond)(remote(X.at[0], X.at[0], xs.at[slot], xr.at[0], device).wait_send)
            for slot in range(3):
                remote(X.at[0], X.at[0], xs.at[3 + slot], xl.at[0], partner).wait_send()

        remote(X, X, xs.at[6], xq.at[0], partner).wait_send()

    @pl.when(core == 1)
    def _():
        mine_1 = L.at[pl.ds(512, 512)]
        give = remote(mine_1, mine_1, ls.at[4], lq.at[0], partner)
        pl.when(src_l)(give.start)
        @pl.when(y == 0)
        def _():
            @pl.loop(0, 7)
            def _(q):
                raw = U[1, :, block(q)]
                value = dot(W[1, 0], raw) + dot(W[1, 1], raw)
                B1[:, block(q)] = value

                @pl.when(q >= SHARED)
                def _():
                    UF[NB : 2 * NB, block(q)] = value.astype(BF16)

            remote(U.at[0], U.at[0], pr.at[0, 0], pr.at[0, 0], partner).wait_recv()
            pl.loop(SHARED, 7)(lambda q: panel(0, q))

        pl.when(y != 0)(lambda: steps(0, LOWER_AT))
        lower()
        pl.when(y != 0)(lambda: steps(LOWER_AT, STEPS))
        corners()
        shared = UF.at[:, pl.ds(0, SHARED * NB)]
        remote(shared, shared, fr.at[0], fr.at[0], partner).wait_recv()

        @pl.when(y == 0)
        def _():
            LF[0:NB] = jnp.zeros((NB, 2 * NB), BF16)

            @pl.loop(0, COLS // NB)
            def _(q):
                cols = block(q)

                @pl.when((q > 0) | (c > 1))
                def _():
                    M[0:NB, cols] = (B1[:, cols] - dot(small[0], UF[0:NB, cols])).astype(BF16)

        for side in range(2):
            for g, (tree, first, count, _, _, _) in enumerate(GROUPS):
                buf = U.at[side, :, pl.ds(first * 64, count * 64)]
                for slot, cond, device in u_children(side, tree):
                    sent = cond if side == 1 else cond & (y != 0)
                    pl.when(sent)(remote(buf, buf, us.at[side, g, slot], ur.at[side, 0], device).wait_send)
            sent = remote(U.at[side], U.at[side], ps.at[side], pr.at[side, 0], partner)
            if side == 1:
                sent.wait_send()
            else:
                pl.when(y != 0)(sent.wait_send)
        pl.when(src_l)(give.wait_send)


def update(UF, LF, M, out, O, sems):
    copies = []
    for q in range(COLS // NB):
        cols = pl.ds(q * NB, NB)
        O[:, cols] = (M[:, cols].astype(F32) - dot(LF[...], UF[:, cols])).astype(BF16)
        copies.append(pltpu.make_async_copy(O.at[:, cols], out.at[:, cols], sems.at[q]))
        copies[-1].start()
    for copy in copies:
        copy.wait()


def body(matrix, lower_inv, upper_inv):
    D = pltpu.SemaphoreType.DMA
    vmem = pl.BlockSpec(memory_space=pltpu.VMEM)
    hbm = pl.BlockSpec(memory_space=pltpu.HBM)
    UF, LF, M = pl.pallas_call(
        gather,
        out_shape=(
            jax.ShapeDtypeStruct((2 * NB, COLS), BF16),
            jax.ShapeDtypeStruct((512, 2 * NB), BF16),
            jax.ShapeDtypeStruct((512, COLS), BF16),
        ),
        in_specs=[hbm] * 3,
        out_specs=(vmem, vmem, vmem),
        scratch_shapes=[
            pltpu.VMEM((2, NB, COLS), BF16),
            pltpu.VMEM((2, NB, NB), BF16),
            pltpu.VMEM((1536, NB), BF16),
            pltpu.VMEM((2, 2, NB, NB), F32),
            pltpu.VMEM((4, 2, NB, NB), BF16),
            pltpu.VMEM((3, NB, NB), BF16),
            pltpu.VMEM((512, NB), F32),
            D((2, 3, 2)),
            D((2, UCH)),
            D((2,)),
            D((2, 7)),
            D((1,)),
            D((1,)),
            D((5,)),
            D((LCH,)),
            D((1,)),
            D((1,)),
            D((7,)),
            D((XCH,)),
            D((2,)),
            D((1,)),
            pltpu.VMEM((NB, COLS), F32),
            pltpu.SemaphoreType.REGULAR((3,)),
            D((5,)),
        ],
        compiler_params=pltpu.CompilerParams(
            collective_id=0, has_side_effects=True, vmem_limit_bytes=32 * 2**20
        ),
    )(*(pltpu.with_memory_space_constraint(a, pltpu.HBM) for a in (matrix, lower_inv, upper_inv)))
    return pl.pallas_call(
        update,
        out_shape=jax.ShapeDtypeStruct(matrix.shape, matrix.dtype),
        in_specs=[vmem] * 3,
        out_specs=hbm,
        scratch_shapes=[pltpu.VMEM((512, COLS), BF16), D((COLS // NB,))],
        compiler_params=pltpu.CompilerParams(vmem_limit_bytes=16 * 2**20),
    )(UF, LF, M)


def solution(mesh):
    in_specs = (P("row", "col"), P(), P())
    return jax.shard_map(body, mesh=mesh, in_specs=in_specs, out_specs=P("row", "col"), check_vma=False)
```

time: 44.4 us -> 37.6 us (0.85)
  the two profiles are of different devices: /device:TPU:120 before, /device:TPU:9 now
where the time goes in v3:
time: 37.6 us; the launch traced here: 37.5 us
  Pallas kernels  37.5 us (100%)
    pallas_call x1, Pallas kernels, body(): pl.pallas_call(gather, out_shape=(jax.ShapeDtypeStruct((2 * NB, COLS), BF...  35.5 us
    pallas_call x1, Pallas kernels, body(): pl.pallas_call(update, out_shape=jax.ShapeDtypeStruct(matrix.shape, matri...  2.02 us

profile of v3, /device:TPU:9, one launch (start us, length us, event | category | flops | bytes accessed | tf_op | source)
XLA Modules:
  0.0 37.5 jit_solution(12394267116218478270)
XLA Ops:
  0.0 35.5 %shard_map.37 = (bf16[512,1792]{1,0:T(8,128)(2,1)S(1)}, bf16[512,512]{1,0:T(8,128)(2,1)S(1)}, bf16[512,1792]{1,0:T(8,128)(2,1)S(1)}) custom-call(bf16[512,1792]{1,0:T(8,128)(2,1)} %mat.1, f32[2,256,256]{2,1,0:T(8,128)} %linv.1, f32[2,256,256]{2,1,0:T(8,128)} %uinv.1), custom_call_target="tpu_custom_call" | custom-call | tf_op jit(solution)/shard_map/pallas_call | solution.py:531
  35.5 2.0 %shard_map.38 = bf16[512,1792]{1,0:T(8,128)(2,1)} custom-call(bf16[512,1792]{1,0:T(8,128)(2,1)S(1)} %get-tuple-element.8.UF, bf16[512,512]{1,0:T(8,128)(2,1)S(1)} %get-tuple-element.9.LF, bf16[512,1792]{1,0:T(8,128)(2,1)S(1)} %get-tuple-element.10.M), custom_call_target="tpu_custom_call" | custom-call | tf_op jit(solution)/shard_map/pallas_call | solution.py:570

commit v4 on v3

--- a/solution.py
+++ b/solution.py
@@ -18,17 +18,19 @@
 LONG = {0: (2,), 2: (3, 1), 3: (4,), 4: (5,), 5: (6,), 6: (7,)}
 
 GROUPS = (
-    (FAR, 0, 4, 0, 1, (0, 8, 5, 8, 11, 8, 5, 8)),
-    (LONG, 4, 16, 4, 2, (-4, 8, 4, 8, 11, 15, 18, 21)),
-    (NEAR, 20, 8, 12, 1, (-8, 4, 7, 10, 14, 10, 7, 4)),
+    (LONG, 0, 4, 0, 2, (0, 8, 5, 8, 11, 15, 18, 21)),
+    (LONG, 4, 16, 2, 2, (0, 8, 5, 8, 11, 15, 18, 21)),
+    (NEAR, 20, 8, 10, 1, (0, 4, 7, 10, 14, 10, 7, 4)),
 )
+FIRST = (FAR, (0, 8, 5, 8, 11, 8, 5, 8))
 UCH = 28
 SHARED = 5
 LROWS = 64
 LCH = 1024 // LROWS
 XCH = NB // LROWS
 STEPS = 36
-LOWER_AT = 30
+LOWER_AT = (28, 24, 28, 28, 23, 28, 28, 24)
+CORNERS_AT = (31, 28, 31, 31, 28, 31, 31, 28)
 PLANE = (0, 10, 6, 10, 15, 10, 6, 10)
 FROM_HUB = (0, 5, 10, 6)
 PLANE_X = (0, 10, 6, 10, 11, 9, 6, 9)
@@ -66,7 +68,7 @@
 
 
 def gather(
-    mat, linv, uinv, UF, LF, M, U, X, L, inv, W, small, D1, us, ur, ps, pr, fs, fr, ls, lr, ll, lq, xs, xr, xl, xq, B1, ready, loc
+    mat, linv, uinv, UF, LF, M, U, X, L, inv, W, small, D1, us, ur, ps, pr, fs, fr, ls, lr, ll, lq, xs, xr, xl, xq, B1, ready, answer, loc
 ):
     r = lax.axis_index("row")
     c = lax.axis_index("col")
@@ -112,7 +114,13 @@
     rank = [[down[(at + off) % NZ].index(-off) for off in d] for at, d in enumerate(up)]
     z_rank = [lut(z, [k[i] if i < len(k) else 0 for k in rank]) for i in range(len(z_up))]
 
-    greet(partner)
+    @pl.when(core == 1)
+    def _():
+        for off in (1, -1, 2, -2):
+            greet(at_y(off, 1))
+        pl.when((y == 1) | (y == 2) | (y == 6) | (y == 7))(lambda: greet((0, c)))
+
+    pl.when(core == 1)(lambda: greet(partner))
     greet(at_x(turn, 0))
 
     @pl.when(first_core)
@@ -122,12 +130,6 @@
         pl.when(x >= 2)(lambda: greet(at_x(-turn, 0)))
         for off in z_down:
             pl.when(hub & (off != 0))(lambda off=off: greet(at_z(off)))
-
-    @pl.when(core == 1)
-    def _():
-        for off in (1, -1, 2, -2):
-            greet(at_y(off, 1))
-        pl.when((y == 1) | (y == 2) | (y == 6) | (y == 7))(lambda: greet((0, c)))
 
     local = [
         pltpu.make_async_copy(linv, inv.at[0], loc.at[1]),
@@ -143,7 +145,29 @@
     pl.when(src_l)(own_cols.start)
     local[2].start()
     count_0 = 3 + jnp.where(hub, 4 + n_up, 0) + jnp.where(y == 0, 4, 0)
-    pl.semaphore_wait(barrier, jnp.where(first_core, count_0, 5))
+    pl.semaphore_wait(barrier, jnp.where(first_core, count_0, 4))
+
+    @pl.when(first_core)
+    def _():
+        pl.semaphore_signal(answer, inc=1, device_id=partner, device_id_type=MESH)
+
+
+    near_side = jnp.where(y <= 4, 0, 1)
+    positions = (y, lax.rem(NY - y, NY))
+    def u_children(side, g):
+        out = []
+        for slot in range(2):
+            offs = offsets(GROUPS[g][0], slot)
+            fast = offsets(FIRST[0], slot) if g == 0 else offs
+            if any(offs) or any(fast):
+                off = lut(positions[side], offs)
+                if g == 0:
+                    off = jnp.where(c == 1 - side, lut(positions[side], fast), off)
+                out.append((slot, off != 0, at_y(off if side == 0 else -off, 1)))
+        return out
+
+    children = [[u_children(side, g) for g in range(len(GROUPS))] for side in range(2)]
+
 
     @pl.when(y == 0)
     def _():
@@ -154,18 +178,14 @@
                 for g, (tree, first, count, _, _, _) in enumerate(GROUPS):
 
                     @pl.loop(first, first + count)
-                    def _(j, g=g, tree=tree):
-                        for slot, child in enumerate(tree[0]):
-                            off = child if child <= 4 else child - 8
-                            remote(
-                                u_part(mat, j),
-                                u_part(U.at[side], j),
-                                us.at[side, g, slot],
-                                ur.at[side, j],
-                                at_y(off if side == 0 else -off, 1),
-                            ).start()
+                    def _(j, g=g):
+                        for slot, cond, device in children[side][g]:
+                            there = u_part(U.at[side], j)
+                            copy = remote(u_part(mat, j), there, us.at[side, g, slot], ur.at[side, j], device)
+                            pl.when(cond)(copy.start)
 
                 if side == 1:
+                    pl.semaphore_wait(answer, 1)
 
                     @pl.loop(0, 7)
                     def _(q):
@@ -191,16 +211,9 @@
     pl.when(src_l)(own_cols.wait)
     local[2].wait()
 
-    positions = (y, lax.rem(NY - y, NY))
-
-    def u_children(side, tree):
-        out = []
-        for slot in range(2):
-            offs = offsets(tree, slot)
-            if any(offs):
-                off = lut(positions[side], offs)
-                out.append((slot, off != 0, at_y(off if side == 0 else -off, 1)))
-        return out
+    @pl.when((core == 1) & (y != 0))
+    def _():
+        pl.semaphore_wait(answer, 1)
 
     def panel(side, q):
         cols = block(q)
@@ -217,7 +230,7 @@
             j = j + first
             buf = u_part(U.at[side], j)
             remote(buf, buf, ur.at[side, j], ur.at[side, j], partner).wait_recv()
-            for slot, cond, device in u_children(side, tree):
+            for slot, cond, device in children[side][g]:
                 pl.when(cond)(remote(buf, buf, us.at[side, g, slot], ur.at[side, j], device).start)
 
             @pl.when(lax.rem(j, 4) == 3)
@@ -227,6 +240,8 @@
                 remote(raw, raw, ps.at[side], pr.at[side, q], partner).start()
                 if first >= 4 * SHARED:
                     panel(side, q)
+                else:
+                    pl.when(side != near_side)(lambda: panel(side, q))
 
         return event
 
@@ -246,7 +261,10 @@
     on_1 = []
     for side in range(2):
         for g, (tree, first, count, start, rate, arrival) in enumerate(GROUPS):
-            on_1.append((start + lut(positions[side], arrival), rate, count // rate, hand_on(side, g, first, tree)))
+            at = lut(positions[side], arrival)
+            if g == 0:
+                at = jnp.where(c == 1 - side, lut(positions[side], FIRST[1]), at)
+            on_1.append((start + at, rate, count // rate, hand_on(side, g, first, tree)))
 
     def rows_of(j, base=0):
         return pl.ds(pl.multiple_of(base + j * LROWS, LROWS), LROWS)
@@ -402,14 +420,10 @@
     @pl.when(first_core)
     def _():
         early = (y == 0) & (z != 0)
-        near_side = jnp.where(y <= 4, 0, 1)
-
-        def first_blocks():
-            take_and_give(0, 0)
-            take_and_give(1, 0)
+        had = jnp.where(src_l, hb, -1)
 
         def near_blocks():
-            pl.loop(1, SHARED)(lambda q: take_and_give(near_side, q))
+            pl.loop(jnp.where(had == near_side, 1, 0), SHARED)(lambda q: take_and_give(near_side, q))
 
         def far_blocks():
             @pl.loop(SHARED, 7)
@@ -417,16 +431,16 @@
                 take(0, q)
                 take(1, q)
 
-            pl.loop(1, SHARED)(lambda q: take_and_give(1 - near_side, q))
+            pl.loop(jnp.where(had == 1 - near_side, 1, 0), SHARED)(lambda q: take(1 - near_side, q))
 
         @pl.when(early)
         def _():
-            first_blocks()
             near_blocks()
             far_blocks()
 
         columns()
-        pl.when(jnp.logical_not(early))(first_blocks)
+        pl.when(had == near_side)(lambda: take_and_give(near_side, 0))
+        pl.when(had == 1 - near_side)(lambda: take(1 - near_side, 0))
 
         @pl.when(hub)
         def _():
@@ -439,10 +453,10 @@
 
         for g, (tree, first, count, _, _, _) in enumerate(GROUPS):
             buf = U.at[0, :, pl.ds(first * 64, count * 64)]
-            for slot, cond, device in u_children(0, tree):
+            for slot, cond, device in children[0][g]:
                 pl.when(cond & (y == 0))(remote(buf, buf, us.at[0, g, slot], ur.at[0, 0], device).wait_send)
         pl.when(y == 0)(remote(U.at[0], U.at[0], ps.at[0], pr.at[0, 0], partner).wait_send)
-        shared = UF.at[:, pl.ds(0, SHARED * NB)]
+        shared = UF.at[0:NB, pl.ds(0, SHARED * NB)]
         remote(shared, shared, fs.at[0], fr.at[0], partner).wait_send()
         whole = L.at[pl.ds(0, 1024)]
         for slot, (cond, device) in enumerate(plane):
@@ -465,6 +479,8 @@
         mine_1 = L.at[pl.ds(512, 512)]
         give = remote(mine_1, mine_1, ls.at[4], lq.at[0], partner)
         pl.when(src_l)(give.start)
+        lower_at, corners_at = lut(y, LOWER_AT), lut(y, CORNERS_AT)
+
         @pl.when(y == 0)
         def _():
             @pl.loop(0, 7)
@@ -473,18 +489,17 @@
                 value = dot(W[1, 0], raw) + dot(W[1, 1], raw)
                 B1[:, block(q)] = value
 
-                @pl.when(q >= SHARED)
-                def _():
-                    UF[NB : 2 * NB, block(q)] = value.astype(BF16)
+                UF[NB : 2 * NB, block(q)] = jnp.where((q > 0) | (c > 1), value, 0.0).astype(BF16)
 
             remote(U.at[0], U.at[0], pr.at[0, 0], pr.at[0, 0], partner).wait_recv()
             pl.loop(SHARED, 7)(lambda q: panel(0, q))
 
-        pl.when(y != 0)(lambda: steps(0, LOWER_AT))
+        pl.when(y != 0)(lambda: steps(0, lower_at))
         lower()
-        pl.when(y != 0)(lambda: steps(LOWER_AT, STEPS))
+        pl.when(y != 0)(lambda: steps(lower_at, corners_at))
         corners()
-        shared = UF.at[:, pl.ds(0, SHARED * NB)]
+        pl.when(y != 0)(lambda: steps(corners_at, STEPS))
+        shared = UF.at[0:NB, pl.ds(0, SHARED * NB)]
         remote(shared, shared, fr.at[0], fr.at[0], partner).wait_recv()
 
         @pl.when(y == 0)
@@ -502,7 +517,7 @@
         for side in range(2):
             for g, (tree, first, count, _, _, _) in enumerate(GROUPS):
                 buf = U.at[side, :, pl.ds(first * 64, count * 64)]
-                for slot, cond, device in u_children(side, tree):
+                for slot, cond, device in children[side][g]:
                     sent = cond if side == 1 else cond & (y != 0)
                     pl.when(sent)(remote(buf, buf, us.at[side, g, slot], ur.at[side, 0], device).wait_send)
             sent = remote(U.at[side], U.at[side], ps.at[side], pr.at[side, 0], partner)
@@ -561,6 +576,7 @@
             D((1,)),
             pltpu.VMEM((NB, COLS), F32),
             pltpu.SemaphoreType.REGULAR((3,)),
+            pltpu.SemaphoreType.REGULAR,
             D((5,)),
         ],
         compiler_params=pltpu.CompilerParams(

time: 37.6 us -> 35.1 us (0.934)
  the two profiles are of different devices: /device:TPU:9 before, /device:TPU:11 now
where the time goes in v4:
time: 35.1 us; the launch traced here: 35 us
  Pallas kernels  35 us (100%)
    pallas_call x1, Pallas kernels, body(): pl.pallas_call(gather, out_shape=(jax.ShapeDtypeStruct((2 * NB, COLS), BF...  32.9 us
    pallas_call x1, Pallas kernels, body(): pl.pallas_call(update, out_shape=jax.ShapeDtypeStruct(matrix.shape, matri...  2.02 us

profile of v4, /device:TPU:11, one launch (start us, length us, event | category | flops | bytes accessed | tf_op | source)
XLA Modules:
  0.0 35.0 jit_solution(5517651303943615555)
XLA Ops:
  0.0 32.9 %shard_map.37 = (bf16[512,1792]{1,0:T(8,128)(2,1)S(1)}, bf16[512,512]{1,0:T(8,128)(2,1)S(1)}, bf16[512,1792]{1,0:T(8,128)(2,1)S(1)}) custom-call(bf16[512,1792]{1,0:T(8,128)(2,1)} %mat.1, f32[2,256,256]{2,1,0:T(8,128)} %linv.1, f32[2,256,256]{2,1,0:T(8,128)} %uinv.1), custom_call_target="tpu_custom_call" | custom-call | tf_op jit(solution)/shard_map/pallas_call | solution.py:546
  33.0 2.0 %shard_map.38 = bf16[512,1792]{1,0:T(8,128)(2,1)} custom-call(bf16[512,1792]{1,0:T(8,128)(2,1)S(1)} %get-tuple-element.8.UF, bf16[512,512]{1,0:T(8,128)(2,1)S(1)} %get-tuple-element.9.LF, bf16[512,1792]{1,0:T(8,128)(2,1)S(1)} %get-tuple-element.10.M), custom_call_target="tpu_custom_call" | custom-call | tf_op jit(solution)/shard_map/pallas_call | solution.py:586

commit v5 on v4

--- a/solution.py
+++ b/solution.py
@@ -18,19 +18,19 @@
 LONG = {0: (2,), 2: (3, 1), 3: (4,), 4: (5,), 5: (6,), 6: (7,)}
 
 GROUPS = (
-    (LONG, 0, 4, 0, 2, (0, 8, 5, 8, 11, 15, 18, 21)),
-    (LONG, 4, 16, 2, 2, (0, 8, 5, 8, 11, 15, 18, 21)),
-    (NEAR, 20, 8, 10, 1, (0, 4, 7, 10, 14, 10, 7, 4)),
+    (LONG, 0, 4, 0, 1, (0, 16, 10, 16, 22, 30, 36, 42)),
+    (LONG, 4, 16, 4, 1, (0, 16, 10, 16, 22, 30, 36, 42)),
+    (NEAR, 20, 8, 20, 2, (0, 8, 14, 20, 28, 20, 14, 8)),
 )
-FIRST = (FAR, (0, 8, 5, 8, 11, 8, 5, 8))
+FIRST = (FAR, (0, 16, 10, 16, 22, 16, 10, 16))
 UCH = 28
 SHARED = 5
 LROWS = 64
 LCH = 1024 // LROWS
 XCH = NB // LROWS
-STEPS = 36
-LOWER_AT = (28, 24, 28, 28, 23, 28, 28, 24)
-CORNERS_AT = (31, 28, 31, 31, 28, 31, 31, 28)
+STEPS = 72
+LOWER_AT = (56, 48, 56, 56, 46, 56, 56, 48)
+CORNERS_AT = (62, 56, 62, 62, 56, 62, 62, 56)
 PLANE = (0, 10, 6, 10, 15, 10, 6, 10)
 FROM_HUB = (0, 5, 10, 6)
 PLANE_X = (0, 10, 6, 10, 11, 9, 6, 9)
@@ -260,11 +260,11 @@
 
     on_1 = []
     for side in range(2):
-        for g, (tree, first, count, start, rate, arrival) in enumerate(GROUPS):
+        for g, (tree, first, count, start, stride, arrival) in enumerate(GROUPS):
             at = lut(positions[side], arrival)
             if g == 0:
                 at = jnp.where(c == 1 - side, lut(positions[side], FIRST[1]), at)
-            on_1.append((start + at, rate, count // rate, hand_on(side, g, first, tree)))
+            on_1.append((start + at, stride, count, hand_on(side, g, first, tree)))
 
     def rows_of(j, base=0):
         return pl.ds(pl.multiple_of(base + j * LROWS, LROWS), LROWS)
@@ -409,13 +409,15 @@
     def steps(begin, end):
         @pl.loop(begin, end)
         def _(it):
-            for start, rate, count, handle in on_1:
+            for start, stride, count, handle in on_1:
                 k = it - start
-
-                @pl.when((k >= 0) & (k < count))
-                def _(k=k, rate=rate, handle=handle):
-                    for i in range(rate):
-                        handle(k * rate + i)
+                ok = (k >= 0) & (k < count * stride)
+                if stride == 2:
+                    ok = ok & (lax.rem(k, 2) == 0)
+
+                @pl.when(ok)
+                def _(k=k, stride=stride, handle=handle):
+                    handle(k // stride if stride > 1 else k)
 
     @pl.when(first_core)
     def _():
@@ -425,13 +427,17 @@
         def near_blocks():
             pl.loop(jnp.where(had == near_side, 1, 0), SHARED)(lambda q: take_and_give(near_side, q))
 
-        def far_blocks():
+        def last_blocks():
             @pl.loop(SHARED, 7)
             def _(q):
                 take(0, q)
                 take(1, q)
 
+        def far_blocks():
+            middle = (y >= 3) & (y <= 5)
+            pl.when(jnp.logical_not(middle))(last_blocks)
             pl.loop(jnp.where(had == 1 - near_side, 1, 0), SHARED)(lambda q: take(1 - near_side, q))
+            pl.when(middle)(last_blocks)
 
         @pl.when(early)
         def _():

time: 35.1 us -> 34.8 us (level)
  Pallas kernels: 35 us -> 34.6 us
where the time goes in v5:
time: 34.8 us; the launch traced here: 34.7 us
  Pallas kernels  34.6 us (99%)
    pallas_call x1, Pallas kernels, body(): pl.pallas_call(gather, out_shape=(jax.ShapeDtypeStruct((2 * NB, COLS), BF...  32.6 us
    pallas_call x1, Pallas kernels, body(): pl.pallas_call(update, out_shape=jax.ShapeDtypeStruct(matrix.shape, matri...  2.03 us

profile of v5, /device:TPU:11, one launch (start us, length us, event | category | flops | bytes accessed | tf_op | source)
XLA Modules:
  0.0 34.7 jit_solution(12325890491218152610)
XLA Ops:
  0.0 32.6 %shard_map.37 = (bf16[512,1792]{1,0:T(8,128)(2,1)S(1)}, bf16[512,512]{1,0:T(8,128)(2,1)S(1)}, bf16[512,1792]{1,0:T(8,128)(2,1)S(1)}) custom-call(bf16[512,1792]{1,0:T(8,128)(2,1)} %mat.1, f32[2,256,256]{2,1,0:T(8,128)} %linv.1, f32[2,256,256]{2,1,0:T(8,128)} %uinv.1), custom_call_target="tpu_custom_call" | custom-call | tf_op jit(solution)/shard_map/pallas_call | solution.py:552
  32.6 2.0 %shard_map.38 = bf16[512,1792]{1,0:T(8,128)(2,1)} custom-call(bf16[512,1792]{1,0:T(8,128)(2,1)S(1)} %get-tuple-element.8.UF, bf16[512,512]{1,0:T(8,128)(2,1)S(1)} %get-tuple-element.9.LF, bf16[512,1792]{1,0:T(8,128)(2,1)S(1)} %get-tuple-element.10.M), custom_call_target="tpu_custom_call" | custom-call | tf_op jit(solution)/shard_map/pallas_call | solution.py:592

commit v6 on v5

--- a/solution.py
+++ b/solution.py
@@ -16,6 +16,7 @@
 FAR = {0: (2, 6), 2: (1, 3), 3: (4,), 6: (7, 5)}
 WIDE = {0: (2, 6), 2: (4, 3, 1), 6: (5, 7)}
 LONG = {0: (2,), 2: (3, 1), 3: (4,), 4: (5,), 5: (6,), 6: (7,)}
+SHORT = {k: v for k, v in LONG.items() if k < 6}
 
 GROUPS = (
     (LONG, 0, 4, 0, 1, (0, 16, 10, 16, 22, 30, 36, 42)),
@@ -157,7 +158,8 @@
     def u_children(side, g):
         out = []
         for slot in range(2):
-            offs = offsets(GROUPS[g][0], slot)
+            tree = GROUPS[g][0]
+            offs = offsets(SHORT if side == 1 and tree is LONG else tree, slot)
             fast = offsets(FIRST[0], slot) if g == 0 else offs
             if any(offs) or any(fast):
                 off = lut(positions[side], offs)
@@ -168,6 +170,14 @@
 
     children = [[u_children(side, g) for g in range(len(GROUPS))] for side in range(2)]
 
+
+    last_groups = [(0, c != 0), (1, c >= 0)]
+
+    def main_sent(side, here):
+        for g, (_, first, count, _, _, _) in enumerate(GROUPS):
+            buf = U.at[side, :, pl.ds(first * 64, count * 64)]
+            for slot, cond, device in children[side][g]:
+                pl.when(cond & here)(remote(buf, buf, us.at[side, g, slot], ur.at[side, 0], device).wait_send)
 
     @pl.when(y == 0)
     def _():
@@ -497,6 +507,16 @@
 
                 UF[NB : 2 * NB, block(q)] = jnp.where((q > 0) | (c > 1), value, 0.0).astype(BF16)
 
+            main_sent(1, y == 0)
+            for g, cond in last_groups:
+
+                @pl.when(cond)
+                def _(g=g):
+                    @pl.loop(GROUPS[g][1], GROUPS[g][1] + GROUPS[g][2])
+                    def _(j):
+                        there = u_part(U.at[1], j)
+                        remote(u_part(mat, j), there, us.at[1, g, 2], ur.at[1, j], at_y(1, 1)).start()
+
             remote(U.at[0], U.at[0], pr.at[0, 0], pr.at[0, 0], partner).wait_recv()
             pl.loop(SHARED, 7)(lambda q: panel(0, q))
 
@@ -520,12 +540,14 @@
                 def _():
                     M[0:NB, cols] = (B1[:, cols] - dot(small[0], UF[0:NB, cols])).astype(BF16)
 
+        @pl.when(y == 0)
+        def _():
+            for g, cond in last_groups:
+                buf = U.at[1, :, pl.ds(GROUPS[g][1] * 64, GROUPS[g][2] * 64)]
+                pl.when(cond)(remote(buf, buf, us.at[1, g, 2], ur.at[1, 0], partner).wait_send)
+
         for side in range(2):
-            for g, (tree, first, count, _, _, _) in enumerate(GROUPS):
-                buf = U.at[side, :, pl.ds(first * 64, count * 64)]
-                for slot, cond, device in children[side][g]:
-                    sent = cond if side == 1 else cond & (y != 0)
-                    pl.when(sent)(remote(buf, buf, us.at[side, g, slot], ur.at[side, 0], device).wait_send)
+            main_sent(side, y != 0)
             sent = remote(U.at[side], U.at[side], ps.at[side], pr.at[side, 0], partner)
             if side == 1:
                 sent.wait_send()
@@ -566,7 +588,7 @@
             pltpu.VMEM((4, 2, NB, NB), BF16),
             pltpu.VMEM((3, NB, NB), BF16),
             pltpu.VMEM((512, NB), F32),
-            D((2, 3, 2)),
+            D((2, 3, 3)),
             D((2, UCH)),
             D((2,)),
             D((2, 7)),

time: 34.8 us -> 34.5 us (level)
  the two profiles are of different devices: /device:TPU:11 before, /device:TPU:19 now
where the time goes in v6:
time: 34.5 us; the launch traced here: 34.4 us
  Pallas kernels  34.3 us (99%)
    pallas_call x1, Pallas kernels, body(): pl.pallas_call(gather, out_shape=(jax.ShapeDtypeStruct((2 * NB, COLS), BF...  32.3 us
    pallas_call x1, Pallas kernels, body(): pl.pallas_call(update, out_shape=jax.ShapeDtypeStruct(matrix.shape, matri...  2.02 us

profile of v6, /device:TPU:19, one launch (start us, length us, event | category | flops | bytes accessed | tf_op | source)
XLA Modules:
  0.0 34.4 jit_solution(5045059584881485779)
XLA Ops:
  0.0 32.3 %shard_map.37 = (bf16[512,1792]{1,0:T(8,128)(2,1)S(1)}, bf16[512,512]{1,0:T(8,128)(2,1)S(1)}, bf16[512,1792]{1,0:T(8,128)(2,1)S(1)}) custom-call(bf16[512,1792]{1,0:T(8,128)(2,1)} %mat.1, f32[2,256,256]{2,1,0:T(8,128)} %linv.1, f32[2,256,256]{2,1,0:T(8,128)} %uinv.1), custom_call_target="tpu_custom_call" | custom-call | tf_op jit(solution)/shard_map/pallas_call | solution.py:574
  32.3 2.0 %shard_map.38 = bf16[512,1792]{1,0:T(8,128)(2,1)} custom-call(bf16[512,1792]{1,0:T(8,128)(2,1)S(1)} %get-tuple-element.8.UF, bf16[512,512]{1,0:T(8,128)(2,1)S(1)} %get-tuple-element.9.LF, bf16[512,1792]{1,0:T(8,128)(2,1)S(1)} %get-tuple-element.10.M), custom_call_target="tpu_custom_call" | custom-call | tf_op jit(solution)/shard_map/pallas_call | solution.py:614
